TPU v7x, 256 devices: a whole 4x4x8 slice. The times are simulated.
256 devices in a mesh: dp: 4 (over y_hi, core), expert: 64 (over z, x, y_lo).
Axes of the slice: x: 4, y: 4 (y_hi: 2, y_lo: 2; y = y_hi * 2 + y_lo), z: 8, core: 2. Of those that a mesh axis runs over, the one named last changes fastest.
Arguments:
- patches: bfloat16 [256, 256, 1024], P(('dp', 'expert')), may hold values from -400 to 400
- router: bfloat16 [1024, 128], replicated, may hold values from -1 to 1
- w_in: bfloat16 [128, 1024, 2560], P('expert', None, 'dp'), may hold values from -0.1875 to 0.1875
- w_out: bfloat16 [128, 2560, 1024], P('expert', 'dp'), may hold values from -0.125 to 0.125
- cotangent: bfloat16 [256, 256, 1024], P(('dp', 'expert')), may hold values from -6 to 6
Outputs:
- mixed: bfloat16 [256, 256, 1024], P(('dp', 'expert'))
- grad_patches: bfloat16 [256, 256, 1024], P(('dp', 'expert'))
- grad_router: bfloat16 [1024, 128], P(('dp', 'expert'))
- grad_w_in: bfloat16 [128, 1024, 2560], P('expert', None, 'dp')
- grad_w_out: bfloat16 [128, 2560, 1024], P('expert', 'dp')
All inputs are finite; a program needn't handle non-finite values.
Results may differ from a plain program's by a relative error of at most 0.013.
Values may be sent and summed in bfloat16 or wider, within the bound.
A program may use at most 64 MiB of HBM per device.

v0:
```python
import math

import jax
import jax.numpy as jnp
from jax import lax
from jax.sharding import PartitionSpec as P

GELU_COEF = math.sqrt(2.0 / math.pi)


def gelu_value(inner):
    return 0.5 * inner * (1.0 + jnp.tanh(GELU_COEF * (inner + 0.044715 * inner * inner * inner)))


def gelu_slope(inner):
    tangent = jnp.tanh(GELU_COEF * (inner + 0.044715 * inner * inner * inner))
    return 0.5 * (1.0 + tangent) + 0.5 * inner * (1.0 - tangent * tangent) * GELU_COEF * (
        1.0 + 3.0 * 0.044715 * inner * inner
    )


def to_experts(values):
    images, experts, features = values.shape
    groups = lax.axis_size("expert")
    arranged = values.reshape(images, groups, experts // groups, features)
    arrived = lax.all_to_all(arranged, "expert", split_axis=1, concat_axis=1, tiled=True)
    gathered = lax.all_gather(arrived, "dp", axis=0, tiled=True)
    return gathered.reshape(lax.axis_size("dp"), images, groups, experts // groups, features)


def to_images(operand, weight, pattern, images, experts, features):
    partial_value = jnp.einsum(pattern, operand, weight, preferred_element_type=jnp.float32)
    arrived = lax.all_to_all(partial_value, "expert", split_axis=2, concat_axis=3, tiled=True)
    summed = lax.psum_scatter(arrived, "dp", scatter_dimension=0, tiled=True)
    return summed.reshape(images, experts, features).astype(jnp.bfloat16)


def on_device(patches, router, w_in, w_out, cotangent):
    images = patches.shape[0]
    features = patches.shape[2]
    experts = router.shape[1]
    logits = jnp.einsum("bmd,de->bme", patches, router, preferred_element_type=jnp.float32)
    dispatch_prob = jax.nn.softmax(logits, axis=1)
    combine_prob = jax.nn.softmax(logits, axis=2)
    dispatch = dispatch_prob.astype(jnp.bfloat16)
    combine = combine_prob.astype(jnp.bfloat16)
    slot_in = jnp.einsum(
        "bme,bmd->bed", dispatch, patches, preferred_element_type=jnp.float32
    ).astype(jnp.bfloat16)
    slot_rows = to_experts(slot_in)
    preact = jnp.einsum("abced,edh->abceh", slot_rows, w_in, preferred_element_type=jnp.float32)
    hidden = gelu_value(preact).astype(jnp.bfloat16)
    slot_out = to_images(hidden, w_out, "abceh,ehd->abced", images, experts, features)
    mixed = jnp.einsum(
        "bme,bed->bmd", combine, slot_out, preferred_element_type=jnp.float32
    ).astype(jnp.bfloat16)
    grad_slot_out = jnp.einsum(
        "bme,bmd->bed", combine, cotangent, preferred_element_type=jnp.float32
    ).astype(jnp.bfloat16)
    grad_combine = jnp.einsum(
        "bmd,bed->bme", cotangent, slot_out, preferred_element_type=jnp.float32
    )
    grad_logit_c = combine_prob * (
        grad_combine - jnp.sum(combine_prob * grad_combine, axis=2, keepdims=True)
    )
    grad_rows = to_experts(grad_slot_out)
    grad_hidden = jnp.einsum(
        "abced,ehd->abceh", grad_rows, w_out, preferred_element_type=jnp.float32
    )
    grad_preact = (grad_hidden * gelu_slope(preact)).astype(jnp.bfloat16)
    grad_w_out = jnp.einsum(
        "abceh,abced->ehd", hidden, grad_rows, preferred_element_type=jnp.float32
    ).astype(jnp.bfloat16)
    grad_w_in = jnp.einsum(
        "abced,abceh->edh", slot_rows, grad_preact, preferred_element_type=jnp.float32
    ).astype(jnp.bfloat16)
    grad_slot_in = to_images(grad_preact, w_in, "abceh,edh->abced", images, experts, features)
    grad_dispatch = jnp.einsum(
        "bmd,bed->bme", patches, grad_slot_in, preferred_element_type=jnp.float32
    )
    grad_logit_d = dispatch_prob * (
        grad_dispatch - jnp.sum(dispatch_prob * grad_dispatch, axis=1, keepdims=True)
    )
    grad_logits = (grad_logit_c + grad_logit_d).astype(jnp.bfloat16)
    grad_patches = jnp.einsum(
        "bme,bed->bmd", dispatch, grad_slot_in, preferred_element_type=jnp.float32
    )
    grad_patches = grad_patches + jnp.einsum(
        "bme,de->bmd", grad_logits, router, preferred_element_type=jnp.float32
    )
    router_term = jnp.einsum(
        "bmd,bme->de", patches, grad_logits, preferred_element_type=jnp.float32
    )
    grad_router = lax.psum_scatter(
        router_term, ("dp", "expert"), scatter_dimension=0, tiled=True
    ).astype(jnp.bfloat16)
    return (mixed, grad_patches.astype(jnp.bfloat16), grad_router, grad_w_in, grad_w_out)


def solution(mesh):
    placed = (
        P(("dp", "expert"), None, None),
        P(),
        P("expert", None, "dp"),
        P("expert", "dp", None),
        P(("dp", "expert"), None, None),
    )
    return jax.shard_map(
        on_device,
        mesh=mesh,
        in_specs=placed,
        out_specs=(
            P(("dp", "expert"), None, None),
            P(("dp", "expert"), None, None),
            P(("dp", "expert"), None),
            P("expert", None, "dp"),
            P("expert", "dp", None),
        ),
        check_vma=False,
    )
```

profile of v0, /device:TPU:1, one launch (start us, length us, event | category | flops | bytes accessed | tf_op | source)
XLA Modules:
  0.0 351.0 jit_solution(4885401067697330104)
XLA Ops:
  7.2 0.0 copy-start
  7.2 0.0 all-gather.3.cloned.1.call-start
  7.2 1.6 fusion.67
  8.8 0.2 fusion.56
  9.0 1.3 convolution_convert_fusion.2
  10.4 0.1 reshape.148
  10.5 24.0 %all_to_all.34 = bf16[1,64,2,1024]{3,2,0,1:T(2,128)(2,1)S(1)} all-to-all(bf16[1,64,2,1024]{3,2,0,1:T(2,128)(2,1)S(1)} %bitcast.127), channel_id=1, replica_groups=mesh['dp'=4,'expert'=64] {'expert'}, dimensions={1} | all-to-all | bytes 524288 | tf_op jit(solution)/shard_map/all_to_all | solution.py:26
  34.4 0.8 copy.41
  35.2 0.0 all-gather.3.cloned.1.call-update
  35.2 0.0 all-gather.5.cloned.1.call-start
  35.3 1.4 convolution_convert_fusion.1
  36.7 0.1 reshape.151
  36.8 16.9 %all_to_all.35 = bf16[1,64,2,1024]{3,2,0,1:T(2,128)(2,1)S(1)} all-to-all(bf16[1,64,2,1024]{3,2,0,1:T(2,128)(2,1)S(1)} %bitcast.128), channel_id=1, replica_groups=mesh['dp'=4,'expert'=64] {'expert'}, dimensions={1} | all-to-all | bytes 524288 | tf_op jit(solution)/shard_map/all_to_all | solution.py:26
  53.7 0.8 copy.45
  54.4 0.0 all-gather.5.cloned.1.call-update
  54.5 0.0 reduce-scatter.6.cloned.1.call-start
  54.5 5.1 %all-gather.3.cloned.1.call-done = bf16[4,64,2,1024]{3,1,0,2:T(8,128)(2,1)} async-done(((bf16[1,64,2,1024]{3,1,0,2:T(8,128)(2,1)}), bf16[4,64,2,1024]{3,1,0,2:T(8,128)(2,1)}) %all-gather.3.cloned.1.call-update) | async-done | bytes 1048592 | tf_op jit(solution)/shard_map/all_gather | solution.py:27
  59.6 0.0 copy-done
  59.6 3.3 fusion.20
  62.9 20.5 %all-gather.5.cloned.1.call-done = bf16[4,64,2,1024]{3,1,0,2:T(8,128)(2,1)} async-done(((bf16[1,64,2,1024]{3,1,0,2:T(8,128)(2,1)}), bf16[4,64,2,1024]{3,1,0,2:T(8,128)(2,1)}) %all-gather.5.cloned.1.call-update) | async-done | bytes 1048592 | tf_op jit(solution)/shard_map/all_gather | solution.py:27
  83.4 3.9 %fusion.32 = bf16[4,64,2,640]{3,1,0,2:T(8,128)(2,1)S(1)} fusion(f32[4,1,64,2,640]{4,2,0,3,1:T(8,128)} %fusion.20, bf16[4,64,2,1024]{3,1,0,2:T(8,128)(2,1)} %all-gather.5.cloned.1.call-done, bf16[2,640,1024]{2,1,0:T(8,128)(2,1)} %param.8), kind=kOutput, calls=%fused_computation.27 | convolution fusion | flops 677314560 | bytes 5636096 | tf_op jit(solution)/shard_map/abced,ehd->abceh/dot_general | solution.py:67
  87.3 1.0 fusion.11
  88.3 1.4 copy.46
  89.7 58.7 %all_to_all.36 = f32[4,1,64,2,1024]{4,0,3,1,2:T(4,128)S(1)} all-to-all(f32[4,1,64,2,1024]{4,0,3,1,2:T(4,128)S(1)} %copy.46), channel_id=1, replica_groups=mesh['dp'=4,'expert'=64] {'expert'}, dimensions={2} | all-to-all | bytes 4194304 | tf_op jit(solution)/shard_map/all_to_all | solution.py:33
  148.4 2.6 copy.47
  151.0 0.0 reduce-scatter.6.cloned.1.call-update
  151.0 0.2 reduce-scatter.4.cloned.1.call-start
  151.2 3.2 fusion.8
  154.4 1.4 copy.42
  155.8 54.6 %all_to_all.37 = f32[4,1,64,2,1024]{4,0,3,1,2:T(4,128)S(1)} all-to-all(f32[4,1,64,2,1024]{4,0,3,1,2:T(4,128)S(1)} %copy.42), channel_id=1, replica_groups=mesh['dp'=4,'expert'=64] {'expert'}, dimensions={2} | all-to-all | bytes 4194304 | tf_op jit(solution)/shard_map/all_to_all | solution.py:33
  210.3 2.5 copy.43
  212.9 0.0 reduce-scatter.4.cloned.1.call-update
  212.9 0.0 copy-start.2
  212.9 0.0 copy-start.9
  212.9 3.9 %bitcast_convert_fusion.1 = bf16[2,1024,640]{2,1,0:T(8,128)(2,1)} fusion(bf16[4,64,2,1024]{3,1,0,2:T(8,128)(2,1)} %all-gather.3.cloned.1.call-done, bf16[4,64,2,640]{3,1,0,2:T(8,128)(2,1)S(1)} %fusion.32), kind=kOutput, calls=%fused_computation.1 | convolution fusion | flops 672399360 | bytes 4325376 | tf_op jit(solution)/shard_map/abced,abceh->edh/dot_general | solution.py:74
  216.8 0.0 copy-done.2
  216.8 0.0 copy-done.9
  216.8 0.0 copy-start.1
  216.8 2.5 bitcast_convert_fusion
  219.3 0.0 reduce-scatter.6.cloned.1.call-done
  219.3 0.0 copy-done.1
  219.3 1.3 convolution_bitcast_fusion.1
  220.7 35.8 %reduce-scatter.4.cloned.1.call-done = f32[1,1,1,128,1024]{4,3,2,1,0:T(8,128)} async-done(((f32[4,1,1,128,1024]{4,3,2,1,0:T(8,128)}), f32[1,1,1,128,1024]{4,3,2,1,0:T(8,128)}) %reduce-scatter.4.cloned.1.call-update) | async-done | bytes 524304 | tf_op jit(solution)/shard_map/reduce_scatter | solution.py:34
  256.5 1.6 multiply_reduce_fusion.1
  258.1 0.0 copy-start.5
  258.1 0.0 copy-start.7
  258.1 0.5 copy-done.5
  258.7 0.0 copy-done.7
  258.7 1.2 convolution_bitcast_fusion
  259.9 0.0 copy-start.3
  259.9 78.7 %all-reduce.2 = bf16[1024,128]{0,1:T(8,128)(2,1)S(1)} all-reduce(f32[1024,128]{0,1:T(8,128)} %convolution_bitcast_fusion), channel_id=4, replica_groups=mesh['dp'=4,'expert'=64] {'dp','expert'}, use_global_device_ids=true, to_apply=%region_8.0.clone | all-reduce | flops 131072 | bytes 786432
  338.6 0.7 dynamic-slice_convert_fusion
  339.3 0.0 copy-start.6
  339.3 0.0 copy-start.8
  339.3 1.4 copy.50
  340.8 1.3 fusion.47
  342.1 0.0 copy-done.3
  342.1 0.0 copy-done.6
  342.1 0.0 copy-done.8
  342.1 0.0 copy-start.4
  342.1 1.2 fusion.36
  343.3 0.0 copy-done.4
  343.3 1.1 fusion.35
Async XLA Ops:
  7.2 52.4 %copy-start = (bf16[2,1024,640]{2,1,0:T(8,128)(2,1)S(1)}, bf16[2,1024,640]{2,1,0:T(8,128)(2,1)}, u32[]{:S(2)}) copy-start(bf16[2,1024,640]{2,1,0:T(8,128)(2,1)} %param.7) | copy-start | bytes 7864324
  7.2 52.4 %all-gather.3.cloned.1.call-start = ((), (), s32[]{:S(2)}) async-start(), calls=%async_computation.6 | async-start | bytes 1310720 | tf_op jit(solution)/shard_map/all_gather | solution.py:27
  35.2 48.1 %all-gather.5.cloned.1.call-start = ((), (), s32[]{:S(2)}) async-start(), calls=%async_computation.8 | async-start | bytes 1310720 | tf_op jit(solution)/shard_map/all_gather | solution.py:27
  54.5 164.9 %reduce-scatter.6.cloned.1.call-start = ((), (), s32[]{:S(2)}) async-start(), calls=%async_computation.9 | async-start | bytes 2621440 | tf_op jit(solution)/shard_map/reduce_scatter | solution.py:34
  151.0 105.5 %reduce-scatter.4.cloned.1.call-start = ((), (), s32[]{:S(2)}) async-start(), calls=%async_computation.7 | async-start | bytes 2621440 | tf_op jit(solution)/shard_map/reduce_scatter | solution.py:34
  212.9 3.9 %copy-start.2 = (f32[4,1,64,2,640]{4,2,0,3,1:T(8,128)S(1)}, f32[4,1,64,2,640]{4,2,0,3,1:T(8,128)}, u32[]{:S(2)}) copy-start(f32[4,1,64,2,640]{4,2,0,3,1:T(8,128)} %fusion.20) | copy-start | bytes 3932164
  212.9 3.9 %copy-start.9 = (bf16[4,64,2,1024]{3,1,0,2:T(8,128)(2,1)S(1)}, bf16[4,64,2,1024]{3,1,0,2:T(8,128)(2,1)}, u32[]{:S(2)}) copy-start(bf16[4,64,2,1024]{3,1,0,2:T(8,128)(2,1)} %all-gather.5.cloned.1.call-done) | copy-start | bytes 3145732
  216.8 2.5 copy-start.1
  258.1 0.6 copy-start.5
  258.1 0.6 copy-start.7
  259.9 82.2 %copy-start.3 = (bf16[1024,128]{1,0:T(8,128)(2,1)S(1)}, bf16[1024,128]{1,0:T(8,128)(2,1)}, u32[]{:S(2)}) copy-start(bf16[1024,128]{1,0:T(8,128)(2,1)} %param.6) | copy-start | bytes 786436
  339.3 2.8 copy-start.6
  339.3 2.8 copy-start.8
  342.1 1.2 copy-start.4
Sparse Core Ops, SparseCore 0:
  35.3 24.2 all-gather.2
  62.0 21.3 all-gather.4
  151.1 48.7 reduce-scatter.5
  213.0 43.4 reduce-scatter.3
where the time goes:
time: 352 us; the launch traced here: 351 us
  blocking collectives  233 us (66%)
  waiting for transfers between devices  61.5 us (17%)
  matrix products  29.9 us (8%)
  between operations  13.9 us (4%)
  local copies, waits for them, and re-layouts  12.2 us (3%)
    all_to_all x2, blocking collectives, to_images(): lax.all_to_all(partial_value, 'expert', split_axis=2, concat_axis=3, tile...  113 us
    unnamed x1, blocking collectives  78.7 us
    all_to_all x2, blocking collectives, to_experts(): lax.all_to_all(arranged, 'expert', split_axis=1, concat_axis=1, tiled=True)  40.8 us
    reduce_scatter x2, waiting for transfers between devices, to_images(): summed = lax.psum_scatter(arrived, 'dp', scatter_dimension=0, tiled=True)  35.8 us
    all_gather x2, waiting for transfers between devices, to_experts(): gathered = lax.all_gather(arrived, 'dp', axis=0, tiled=True)  25.6 us
  transfers between devices with their start and end apart: 4, of which 3 were waited for; matrix products, arithmetic and copies ran while one was open for 6% of the time, Pallas kernels for 0%

commit v1 on v0

v1 whole, which is shorter than its diff:
```python
import math

import jax
import jax.numpy as jnp
from jax import lax
from jax.experimental import pallas as pl
from jax.experimental.pallas import tpu as pltpu
from jax.sharding import PartitionSpec as P

MESH = pl.DeviceIdType.MESH
GELU_COEF = math.sqrt(2.0 / math.pi)
F32 = jnp.float32
BF16 = jnp.bfloat16
D, FF, M, E = 1024, 640, 256, 128
NC = 4
W = D // NC


def dot(a, b):
    return jnp.dot(a, b, preferred_element_type=F32)


def dot_t(a, b):
    return lax.dot_general(a, b, (((1,), (1,)), ((), ())), preferred_element_type=F32)


def dot_tl(a, b):
    return lax.dot_general(a, b, (((0,), (0,)), ((), ())), preferred_element_type=F32)


def one_hot(rows, columns, old_of_new):
    new = lax.broadcasted_iota(jnp.int32, (rows, columns), 0)
    old = lax.broadcasted_iota(jnp.int32, (rows, columns), 1)
    return jnp.where(old_of_new(new) == old, 1.0, 0.0).astype(BF16)


def kernel(
    patches_hbm, router_hbm, w_in_hbm, w_out_hbm, cot_hbm,
    mixed_hbm, gp_hbm, gr_ref, gwi_hbm, gwo_hbm,
    patches, router, w_in, w_out, cot, mixed, gp, gwi, gwo,
    perm, pt, router_t, prob_d, prob_c, disp_t, disp, comb,
    s_buf, x1, x2, x3, x4, xf, pre, slope, hid, gpre,
    po, cs, cr, ys, yr, zs, zr, ws, wr, grad_c, grad_d,
    rt, rcs, rcr, rys, ryr, rzs, rzr, rxr,
    in_sem, out_sem, fs_sem, fr_sem, bs_sem, br_sem, rs_sem, rr_sem,
):
    dp = lax.axis_index("dp")
    ex = lax.axis_index("expert")
    yh, c = dp // 2, dp % 2
    z, x, yl = ex // 8, (ex // 2) % 4, ex % 2
    y = yh * 2 + yl

    def at(x=x, y=y, z=z, c=c):
        return {"dp": (y // 2) * 2 + c, "expert": (z * 4 + x) * 2 + y % 2}

    x_ids = [(x + k) % 4 for k in range(1, 4)]
    y_ids = [(y + k) % 4 for k in range(1, 4)]
    z_ids = [(z + k) % 8 for k in range(1, 8)]

    barrier = pltpu.get_barrier_semaphore()
    everyone = (
        [at(x=v) for v in x_ids] + [at(y=v) for v in y_ids]
        + [at(z=v) for v in z_ids] + [at(c=1 - c)]
    )
    for other in everyone:
        pl.semaphore_signal(barrier, inc=1, device_id=other, device_id_type=MESH)

    loads = [
        pltpu.make_async_copy(src, dst, in_sem.at[i])
        for i, (src, dst) in enumerate(
            [(patches_hbm, patches), (router_hbm, router), (cot_hbm, cot), (w_in_hbm, w_in), (w_out_hbm, w_out)]
        )
    ]
    for load in loads:
        load.start()

    def send(src, dst, ssem, rsem, other):
        pltpu.make_async_remote_copy(
            src_ref=src, dst_ref=dst, send_sem=ssem, recv_sem=rsem, device_id=other, device_id_type=MESH
        ).start()

    def wait(ref, sem):
        pltpu.make_async_copy(ref, ref, sem).wait()

    def rows(start, size):
        return pl.ds(pl.multiple_of(start, size), size)

    def cols(k):
        return slice(k * W, (k + 1) * W)

    perm[0] = one_hot(E, E, lambda i: (i % 4) * 32 + (i // 16) * 4 + (i // 4) % 4)
    perm[1] = one_hot(E, E, lambda i: ((i // 4) % 8) * 16 + (i // 32) * 4 + i % 4)
    perm[2] = one_hot(E, E, lambda i: ((i // 4) % 8) * 16 + (i % 4) * 4 + i // 32)
    perm[3] = one_hot(E, E, lambda i: ((i // 4) % 4) * 32 + (i // 16) * 4 + i % 4)
    perm[4] = one_hot(E, E, lambda i: ((i // 4) % 8) * 16 + (i // 32) * 4 + i % 4)

    loads[1].wait()
    router_t[...] = dot_t(perm[4], router[...]).astype(BF16)
    loads[0].wait()
    logits = dot_t(router_t[...], patches[...])
    e_d = jnp.exp(logits - jnp.max(logits, axis=1, keepdims=True))
    p_d = e_d / jnp.sum(e_d, axis=1, keepdims=True)
    prob_d[...] = p_d
    disp_t[0] = p_d.astype(BF16)

    def f0(p, k):
        rhs = patches if p == 0 else cot
        s_buf[p, k] = dot(disp_t[p], rhs[:, cols(k)]).astype(BF16)

    def f1(p, k):
        for v in x_ids:
            send(s_buf.at[p, k, rows(v * 32, 32)], x1.at[p, k, rows(x * 32, 32)], fs_sem.at[p, k, 0], fr_sem.at[p, k, 0], at(x=v))
        x1[p, k, rows(x * 32, 32), :] = s_buf[p, k, rows(x * 32, 32), :]

    def f2(p, k):
        wait(x1.at[p, k, pl.ds(0, 96)], fr_sem.at[p, k, 0])
        x2[p, k] = dot(perm[0], x1[p, k]).astype(BF16)
        for v in z_ids:
            send(x2.at[p, k, rows(v * 16, 16)], x3.at[p, k, rows(z * 16, 16)], fs_sem.at[p, k, 1], fr_sem.at[p, k, 1], at(z=v))
        x3[p, k, rows(z * 16, 16), :] = x2[p, k, rows(z * 16, 16), :]

    def f3(p, k):
        wait(x3.at[p, k, pl.ds(0, 112)], fr_sem.at[p, k, 1])
        x4[p, k] = dot(perm[1], x3[p, k]).astype(BF16).reshape(4, 32, W)
        mine = rows(c * 128 + y * 32, 32)
        for v in y_ids:
            send(x4.at[p, k, pl.ds((v % 2) * 2, 2)], xf.at[p, k, :, mine], fs_sem.at[p, k, 2], fr_sem.at[p, k, 2], at(y=v))
        for s in range(2):
            xf[p, k, s, mine, :] = x4[p, k, yl * 2 + s]

    def f4(p, k):
        wait(xf.at[p, k, :, pl.ds(0, 96)], fr_sem.at[p, k, 2])
        half = xf.at[p, k, :, rows(c * 128, 128)]
        send(half, half, fs_sem.at[p, k, 3], fr_sem.at[p, k, 3], at(c=1 - c))

    def f5(p, k):
        wait(xf.at[p, k, :, pl.ds(0, 128)], fr_sem.at[p, k, 3])
        for s in range(2):
            if p == 0:
                term = dot(xf[0, k, s], w_in[s, cols(k), :])
            else:
                term = dot_t(xf[1, k, s], w_out[s, :, cols(k)])
            if k == 0:
                pre[p, s] = term
            else:
                pre[p, s] += term

    def gelu():
        for s in range(2):
            def block(i, carry):
                r = rows(i * 32, 32)
                v = pre[0, s, r, :]
                t = jnp.tanh(GELU_COEF * (v + 0.044715 * v * v * v))
                hid[s, r, :] = (0.5 * v * (1.0 + t)).astype(BF16)
                slope[s, r, :] = 0.5 * (1.0 + t) + 0.5 * v * (1.0 - t * t) * GELU_COEF * (1.0 + 3.0 * 0.044715 * v * v)
                return carry
            lax.fori_loop(0, 8, block, 0)

    def grad_pre():
        for s in range(2):
            def block(i, carry):
                r = rows(i * 32, 32)
                gpre[s, r, :] = (pre[1, s, r, :] * slope[s, r, :]).astype(BF16)
                return carry
            lax.fori_loop(0, 8, block, 0)

    def g1(p, k):
        for s in range(2):
            if p == 0:
                po[p, k, s] = dot(hid[s], w_out[s, :, cols(k)])
            else:
                po[p, k, s] = dot_t(gpre[s], w_in[s, cols(k), :])
            cs[p, k, s] = po[p, k, s, rows((1 - c) * 128, 128), :].astype(BF16)
        send(cs.at[p, k], cr.at[p, k], bs_sem.at[p, k, 0], br_sem.at[p, k, 0], at(c=1 - c))

    def g2(p, k):
        wait(cr.at[p, k], br_sem.at[p, k, 0])
        for s in range(2):
            total = (po[p, k, s, rows(c * 128, 128), :] + cr[p, k, s].astype(F32)).astype(BF16)
            for v in range(4):
                ys[p, k, v, s] = total[v * 32:(v + 1) * 32]
        for v in y_ids:
            send(ys.at[p, k, v], yr.at[p, k, y], bs_sem.at[p, k, 1], br_sem.at[p, k, 1], at(y=v))
        yr[p, k, y] = ys[p, k, y]

    def g3(p, k):
        wait(yr.at[p, k, pl.ds(0, 3)], br_sem.at[p, k, 1])
        total = (yr[p, k, 0:2].astype(F32) + yr[p, k, 2:4].astype(F32)).astype(BF16).reshape(E, W)
        zs[p, k] = dot(perm[3], total).astype(BF16)
        for v in z_ids:
            send(zs.at[p, k, rows(v * 16, 16)], zr.at[p, k, rows(z * 16, 16)], bs_sem.at[p, k, 2], br_sem.at[p, k, 2], at(z=v))
        zr[p, k, rows(z * 16, 16), :] = zs[p, k, rows(z * 16, 16), :]

    def g4(p, k):
        wait(zr.at[p, k, pl.ds(0, 112)], br_sem.at[p, k, 2])
        ws[p, k] = dot(perm[2], zr[p, k]).astype(BF16)
        for v in x_ids:
            send(ws.at[p, k, rows(v * 32, 32)], wr.at[p, k, rows(x * 32, 32)], bs_sem.at[p, k, 3], br_sem.at[p, k, 3], at(x=v))
        wr[p, k, rows(x * 32, 32), :] = ws[p, k, rows(x * 32, 32), :]

    def g5(p, k):
        wait(wr.at[p, k, pl.ds(0, 96)], br_sem.at[p, k, 3])
        if p == 0:
            mixed[:, cols(k)] = dot(comb[...], wr[0, k]).astype(BF16)
            term = dot_t(wr[0, k], cot[:, cols(k)])
            acc = grad_c
        else:
            term = dot_t(wr[1, k], patches[:, cols(k)])
            acc = grad_d
        if k == 0:
            acc[...] = term
        else:
            acc[...] += term

    def w_out_grad(k):
        for s in range(2):
            gwo[s, :, cols(k)] = dot_tl(hid[s], xf[1, k, s]).astype(BF16)

    def w_in_grad(k):
        for s in range(2):
            gwi[s, cols(k), :] = dot_tl(xf[0, k, s], gpre[s]).astype(BF16)

    def combine_probs():
        e_c = jnp.exp(logits - jnp.max(logits, axis=0, keepdims=True))
        p_c = e_c / jnp.sum(e_c, axis=0, keepdims=True)
        prob_c[...] = p_c
        disp_t[1] = p_c.astype(BF16)

    def images_side():
        disp[...] = disp_t[0].T
        comb[...] = disp_t[1].T
        pick = one_hot(M, M, lambda i: ((i // 16) % 8) * 32 + ((i // 4) % 4) * 8 + (i // 128) * 4 + i % 4)
        for cc in range(2):
            for hh in range(2):
                pt[cc * 512 + hh * 256:cc * 512 + (hh + 1) * 256] = dot_t(
                    pick, patches[:, hh * 512 + cc * 256:hh * 512 + (cc + 1) * 256]
                ).astype(BF16)

    outs = {}

    def put(name, src, dst, i):
        outs[name] = pltpu.make_async_copy(src, dst, out_sem.at[i])
        outs[name].start()

    for k in range(NC):
        f0(0, k)
        if k == 0:
            pl.semaphore_wait(barrier, len(everyone))
        f1(0, k)
    combine_probs()
    loads[2].wait()
    f0(1, 0)
    f0(1, 1)
    f0(1, 2)
    f0(1, 3)
    f2(0, 0)
    f2(0, 1)
    f2(0, 2)
    f2(0, 3)
    f3(0, 0)
    f1(1, 0)
    f3(0, 1)
    f1(1, 1)
    f4(0, 0)
    f3(0, 2)
    f1(1, 2)
    f4(0, 1)
    f3(0, 3)
    f1(1, 3)
    images_side()
    f2(1, 0)
    f4(0, 2)
    f2(1, 1)
    loads[3].wait()
    f5(0, 0)
    f4(0, 3)
    f2(1, 2)
    f5(0, 1)
    f3(1, 0)
    f5(0, 2)
    f2(1, 3)
    f5(0, 3)
    gelu()
    loads[4].wait()
    g1(0, 0)
    f3(1, 1)
    f4(1, 0)
    g1(0, 1)
    g2(0, 0)
    f3(1, 2)
    f4(1, 1)
    g1(0, 2)
    g2(0, 1)
    f3(1, 3)
    f4(1, 2)
    f5(1, 0)
    g1(0, 3)
    g2(0, 2)
    f4(1, 3)
    g3(0, 0)
    f5(1, 1)
    g2(0, 3)
    g3(0, 1)
    f5(1, 2)
    f5(1, 3)
    grad_pre()
    g1(1, 0)
    g3(0, 2)
    g1(1, 1)
    g2(1, 0)
    g3(0, 3)
    g1(1, 2)
    g2(1, 1)
    g4(0, 0)
    g1(1, 3)
    g2(1, 2)
    g4(0, 1)
    g3(1, 0)
    g2(1, 3)
    g4(0, 2)
    w_out_grad(0)
    w_out_grad(1)
    g3(1, 1)
    g4(0, 3)
    w_out_grad(2)
    w_out_grad(3)
    g3(1, 2)
    put("gwo", gwo, gwo_hbm, 0)
    g5(0, 0)
    g5(0, 1)
    g3(1, 3)
    g5(0, 2)
    g5(0, 3)
    put("mixed", mixed, mixed_hbm, 1)
    g4(1, 0)
    w_in_grad(0)
    g4(1, 1)
    w_in_grad(1)
    g4(1, 2)
    w_in_grad(2)
    w_in_grad(3)
    put("gwi", gwi, gwi_hbm, 2)
    p_c = prob_c[...]
    g_c = grad_c[...]
    grad_c[...] = p_c * (g_c - jnp.sum(p_c * g_c, axis=0, keepdims=True))
    g4(1, 3)
    g5(1, 0)
    g5(1, 1)
    g5(1, 2)
    g5(1, 3)
    p_d = prob_d[...]
    g_d = grad_d[...]
    g_t = (grad_c[...] + p_d * (g_d - jnp.sum(p_d * g_d, axis=1, keepdims=True))).astype(BF16)

    rt[...] = dot_t(pt[...], g_t)
    rcs[...] = rt[rows((1 - c) * 512, 512), :].astype(BF16)
    send(rcs, rcr, rs_sem.at[0], rr_sem.at[0], at(c=1 - c))
    g_m = g_t.T
    for k in range(2):
        gp[:, cols(k)] = (dot(disp[...], wr[1, k]) + dot(g_m, router_t[:, cols(k)])).astype(BF16)
    wait(rcr, rr_sem.at[0])
    rys[...] = (rt[rows(c * 512, 512), :] + rcr[...].astype(F32)).astype(BF16).reshape(4, 128, 128)
    for v in y_ids:
        send(rys.at[v], ryr.at[y], rs_sem.at[1], rr_sem.at[1], at(y=v))
    ryr[y] = rys[y]
    for k in range(2, 4):
        gp[:, cols(k)] = (dot(disp[...], wr[1, k]) + dot(g_m, router_t[:, cols(k)])).astype(BF16)
    put("gp", gp, gp_hbm, 3)
    wait(ryr.at[pl.ds(0, 3)], rr_sem.at[1])
    rzs[...] = jnp.sum(ryr[...].astype(F32), axis=0).reshape(8, 16, 128)
    for v in z_ids:
        send(rzs.at[v], rzr.at[z], rs_sem.at[2], rr_sem.at[2], at(z=v))
    rzr[z] = rzs[z]
    wait(rzr.at[pl.ds(0, 7)], rr_sem.at[2])
    rxr[x] = jnp.sum(rzr[...], axis=0)
    for v in x_ids:
        send(rxr.at[x], rxr.at[x], rs_sem.at[3], rr_sem.at[3], at(x=v))
    wait(rxr.at[pl.ds(0, 3)], rr_sem.at[3])
    total = jnp.sum(rxr[...], axis=0).astype(BF16)
    total = dot(total, perm[4])
    mine = jnp.zeros((4, E), F32)
    for v in range(4):
        mine = jnp.where(x == v, total[v * 4:(v + 1) * 4], mine)
    gr_ref[...] = mine.astype(BF16)

    for p in range(2):
        for k in range(NC):
            wait(x1.at[p, k, pl.ds(0, 96)], fs_sem.at[p, k, 0])
            wait(x3.at[p, k, pl.ds(0, 112)], fs_sem.at[p, k, 1])
            wait(xf.at[p, k, :, pl.ds(0, 96)], fs_sem.at[p, k, 2])
            wait(xf.at[p, k, :, pl.ds(0, 128)], fs_sem.at[p, k, 3])
            wait(cr.at[p, k], bs_sem.at[p, k, 0])
            wait(yr.at[p, k, pl.ds(0, 3)], bs_sem.at[p, k, 1])
            wait(zr.at[p, k, pl.ds(0, 112)], bs_sem.at[p, k, 2])
            wait(wr.at[p, k, pl.ds(0, 96)], bs_sem.at[p, k, 3])
    wait(rcr, rs_sem.at[0])
    wait(ryr.at[pl.ds(0, 3)], rs_sem.at[1])
    wait(rzr.at[pl.ds(0, 7)], rs_sem.at[2])
    wait(rxr.at[pl.ds(0, 3)], rs_sem.at[3])
    for name in outs:
        outs[name].wait()


def on_device(patches, router, w_in, w_out, cotangent):
    v = pltpu.VMEM
    any_spec = pl.BlockSpec(memory_space=pl.ANY)
    shape = jax.ShapeDtypeStruct
    mixed, gp, gr, gwi, gwo = pl.pallas_call(
        kernel,
        name="soft_moe",
        out_shape=(
            shape((M, D), BF16), shape((M, D), BF16), shape((4, E), BF16), shape((2, D, FF), BF16), shape((2, FF, D), BF16),
        ),
        in_specs=[any_spec] * 5,
        out_specs=(any_spec, any_spec, pl.BlockSpec(memory_space=pltpu.VMEM), any_spec, any_spec),
        scratch_shapes=[
            v((M, D), BF16), v((D, E), BF16), v((2, D, FF), BF16), v((2, FF, D), BF16), v((M, D), BF16),
            v((M, D), BF16), v((M, D), BF16), v((2, D, FF), BF16), v((2, FF, D), BF16),
            v((5, E, E), BF16), v((D, M), BF16), v((E, D), BF16), v((E, M), F32), v((E, M), F32),
            v((2, E, M), BF16), v((M, E), BF16), v((M, E), BF16),
            v((2, NC, E, W), BF16), v((2, NC, E, W), BF16), v((2, NC, E, W), BF16), v((2, NC, E, W), BF16),
            v((2, NC, 4, 32, W), BF16), v((2, NC, 2, 256, W), BF16),
            v((2, 2, 256, FF), F32), v((2, 256, FF), F32), v((2, 256, FF), BF16), v((2, 256, FF), BF16),
            v((2, NC, 2, 256, W), F32), v((2, NC, 2, 128, W), BF16), v((2, NC, 2, 128, W), BF16),
            v((2, NC, 4, 2, 32, W), BF16), v((2, NC, 4, 2, 32, W), BF16),
            v((2, NC, E, W), BF16), v((2, NC, E, W), BF16), v((2, NC, E, W), BF16), v((2, NC, E, W), BF16),
            v((E, M), F32), v((E, M), F32),
            v((D, E), F32), v((512, E), BF16), v((512, E), BF16), v((4, 128, E), BF16), v((4, 128, E), BF16),
            v((8, 16, E), F32), v((8, 16, E), F32), v((4, 16, E), F32),
            pltpu.SemaphoreType.DMA((5,)), pltpu.SemaphoreType.DMA((4,)),
            pltpu.SemaphoreType.DMA((2, NC, 4)), pltpu.SemaphoreType.DMA((2, NC, 4)),
            pltpu.SemaphoreType.DMA((2, NC, 4)), pltpu.SemaphoreType.DMA((2, NC, 4)),
            pltpu.SemaphoreType.DMA((4,)), pltpu.SemaphoreType.DMA((4,)),
        ],
        compiler_params=pltpu.CompilerParams(
            collective_id=0, has_side_effects=True, vmem_limit_bytes=50 * 2**20
        ),
        cost_estimate=pl.CostEstimate(flops=4_700_000_000, bytes_accessed=13_000_000, transcendentals=500_000),
    )(patches[0], router, w_in, w_out, cotangent[0])
    return mixed[None], gp[None], gr, gwi, gwo


def solution(mesh):
    placed = (
        P(("dp", "expert"), None, None),
        P(),
        P("expert", None, "dp"),
        P("expert", "dp", None),
        P(("dp", "expert"), None, None),
    )
    return jax.shard_map(
        on_device,
        mesh=mesh,
        in_specs=placed,
        out_specs=(
            P(("dp", "expert"), None, None),
            P(("dp", "expert"), None, None),
            P(("dp", "expert"), None),
            P("expert", None, "dp"),
            P("expert", "dp", None),
        ),
        check_vma=False,
    )
```

time: 352 us -> 92.9 us (0.26)
  blocking collectives: 233 us -> 0 us
  Pallas kernels: 0 us -> 81.8 us
  waiting for transfers between devices: 61.5 us -> 0 us
  matrix products: 29.9 us -> 0 us
  between operations: 13.9 us -> 0.65 us
    all_to_all x4 -> x0, blocking collectives: 154 us -> none  [the longest x2 113 us: to_images(): lax.all_to_all(partial_value, 'expert', split_axis=2, concat_axis=3, tile...]
    pallas_call x0 -> x1, Pallas kernels: none -> 81.8 us  [on_device(): pl.pallas_call(kernel, name='soft_moe', out_shape=(shape((M, D), BF16), s...]
    unnamed x1 -> x0, blocking collectives: 78.7 us -> none
    reduce_scatter x2 -> x0, waiting for transfers between devices: 35.8 us -> none  [to_images(): summed = lax.psum_scatter(arrived, 'dp', scatter_dimension=0, tiled=True)]
    dot_general x15 -> x0, matrix products: 29.9 us -> none  [the longest x2 4.19 us: to_images(): jnp.einsum(pattern, operand, weight, preferred_element_type=jnp.float32)]
    all_gather x2 -> x0, waiting for transfers between devices: 25.6 us -> none  [to_experts(): gathered = lax.all_gather(arrived, 'dp', axis=0, tiled=True)]
    unnamed x21 -> x13, local copies, waits for them, and re-layouts: 2.04 us -> 10.3 us
    all_to_all x4 -> x0, local copies, waits for them, and re-layouts: 6.59 us -> none  [the longest x2 5.08 us: to_images(): lax.all_to_all(partial_value, 'expert', split_axis=2, concat_axis=3, tile...]
  transfers between devices with their start and end apart: 4 -> 0, of which waited for: 3 -> 0; matrix products, arithmetic and copies ran while one was open for 6% -> 0% of each run, Pallas kernels for 0% -> 0%
where the time goes in v1:
time: 92.9 us; the launch traced here: 92.7 us
  Pallas kernels  81.8 us (88%)
  local copies, waits for them, and re-layouts  10.3 us (11%)
    pallas_call x1, Pallas kernels, on_device(): pl.pallas_call(kernel, name='soft_moe', out_shape=(shape((M, D), BF16), s...  81.8 us
    unnamed x13, local copies, waits for them, and re-layouts  10.3 us

profile of v1, /device:TPU:1, one launch (start us, length us, event | category | flops | bytes accessed | tf_op | source)
XLA Modules:
  0.0 92.7 jit_solution(10958447969844736876)
XLA Ops:
  0.6 0.0 copy-start
  0.6 1.0 %copy-done = bf16[1,256,1024]{2,1,0:T(8,128)(2,1)S(1)} copy-done((bf16[1,256,1024]{2,1,0:T(8,128)(2,1)S(1)}, bf16[1,256,1024]{2,1,0:T(8,128)(2,1)}, u32[]{:S(2)}) %copy-start) | copy-done | bytes 524312
  1.7 0.0 copy-start.1
  1.7 1.0 %copy-done.1 = bf16[1,256,1024]{2,1,0:T(8,128)(2,1)S(1)} copy-done((bf16[1,256,1024]{2,1,0:T(8,128)(2,1)S(1)}, bf16[1,256,1024]{2,1,0:T(8,128)(2,1)}, u32[]{:S(2)}) %copy-start.1) | copy-done | bytes 524312
  2.7 0.0 copy-start.2
  2.7 0.9 %copy-done.2 = bf16[1024,128]{1,0:T(8,128)(2,1)S(1)} copy-done((bf16[1024,128]{1,0:T(8,128)(2,1)S(1)}, bf16[1024,128]{1,0:T(8,128)(2,1)}, u32[]{:S(2)}) %copy-start.2) | copy-done | bytes 262168
  3.7 81.8 %soft_moe.1 = (bf16[256,1024]{1,0:T(8,128)(2,1)S(1)}, bf16[256,1024]{1,0:T(8,128)(2,1)S(1)}, bf16[4,128]{1,0:T(4,128)(2,1)S(1)}, bf16[2,1024,640]{2,1,0:T(8,128)(2,1)}, bf16[2,640,1024]{2,1,0:T(8,128)(2,1)}) custom-call(bf16[256,1024]{1,0:T(8,128)(2,1)S(1)} %bitcast.6, bf16[1024,128]{1,0:T(8,128)(2,1)S(1)} %copy-done.2, bf16[2,1024,640]{2,1,0:T(8,128)(2,1)} %w_in_hbm.1, ...), custom_call_target="tpu_custom_call" | custom-call | flops 4700000256 | bytes 13000000 | tf_op jit(solution)/shard_map/soft_moe/pallas_call | solution.py:408
  85.4 0.8 copy.15
  86.2 0.8 copy.16
  87.0 0.6 copy.17
  87.6 0.0 copy-start.3
  87.6 3.6 %copy.18 = bf16[2,1024,640]{2,1,0:T(8,128)(2,1)} copy(bf16[2,1024,640]{2,1,0:T(8,128)(2,1)} %get-tuple-element.23) | data formatting | bytes 5242880
  91.2 0.0 copy-done.3
  91.2 1.5 %copy.19 = bf16[2,640,1024]{2,1,0:T(8,128)(2,1)} copy(bf16[2,640,1024]{2,1,0:T(8,128)(2,1)S(1)} %copy-done.3) | data formatting | bytes 5242880
Async XLA Ops:
  0.6 1.0 %copy-start = (bf16[1,256,1024]{2,1,0:T(8,128)(2,1)S(1)}, bf16[1,256,1024]{2,1,0:T(8,128)(2,1)}, u32[]{:S(2)}) copy-start(bf16[1,256,1024]{2,1,0:T(8,128)(2,1)} %param.5) | copy-start | bytes 1572868
  1.7 1.0 %copy-start.1 = (bf16[1,256,1024]{2,1,0:T(8,128)(2,1)S(1)}, bf16[1,256,1024]{2,1,0:T(8,128)(2,1)}, u32[]{:S(2)}) copy-start(bf16[1,256,1024]{2,1,0:T(8,128)(2,1)} %param.9) | copy-start | bytes 1572868
  2.7 0.9 %copy-start.2 = (bf16[1024,128]{1,0:T(8,128)(2,1)S(1)}, bf16[1024,128]{1,0:T(8,128)(2,1)}, u32[]{:S(2)}) copy-start(bf16[1024,128]{1,0:T(8,128)(2,1)} %router_hbm.1) | copy-start | bytes 786436
  87.6 3.6 %copy-start.3 = (bf16[2,640,1024]{2,1,0:T(8,128)(2,1)S(1)}, bf16[2,640,1024]{2,1,0:T(8,128)(2,1)}, u32[]{:S(2)}) copy-start(bf16[2,640,1024]{2,1,0:T(8,128)(2,1)} %get-tuple-element.24) | copy-start | bytes 7864324

commit v2 on v0

v2 whole, which is shorter than its diff:
```python
import math

import jax
import jax.numpy as jnp
from jax import lax
from jax.experimental import pallas as pl
from jax.experimental.pallas import tpu as pltpu
from jax.sharding import PartitionSpec as P

MESH = pl.DeviceIdType.MESH
GELU_COEF = math.sqrt(2.0 / math.pi)
F32 = jnp.float32
BF16 = jnp.bfloat16
D, FF, M, E = 1024, 640, 256, 128
W = 256


def dot(a, b):
    return jnp.dot(a, b, preferred_element_type=F32)


def dot_t(a, b):
    return lax.dot_general(a, b, (((1,), (1,)), ((), ())), preferred_element_type=F32)


def dot_tl(a, b):
    return lax.dot_general(a, b, (((0,), (0,)), ((), ())), preferred_element_type=F32)


def one_hot(rows, columns, old_of_new):
    new = lax.broadcasted_iota(jnp.int32, (rows, columns), 0)
    old = lax.broadcasted_iota(jnp.int32, (rows, columns), 1)
    return jnp.where(old_of_new(new) == old, 1.0, 0.0).astype(BF16)


GROUPS = ((0, 1, 7, 2), (6, 3, 5, 4))


def kernel(
    patches_hbm, router_hbm, w_in_hbm, w_out_hbm, cot_hbm,
    mixed, gp, gr_ref, gwi, gwo,
    patches, router, w_in, w_out, cot,
    perm, pt, router_t, prob_d, prob_c, disp_t, disp, comb,
    sr, ms, xr, x4, xf, pre, slope, hid, gpre,
    po, cs, cr, ys, yr, zs, zr, so, grad_c, grad_d,
    rt, rcs, rcr, rys, ryr, rzs, rzr,
    in_sem, fs_sem, fr_sem, bs_sem, br_sem, rs_sem, rr_sem,
):
    dp = lax.axis_index("dp")
    ex = lax.axis_index("expert")
    yh, c = dp // 2, dp % 2
    z, x, yl = ex // 8, (ex // 2) % 4, ex % 2
    y = yh * 2 + yl

    def at(x=x, y=y, z=z, c=c):
        return {"dp": (y // 2) * 2 + c, "expert": (z * 4 + x) * 2 + y % 2}

    y_ids = [(y + k) % 4 for k in range(1, 4)]
    plane = [
        (g, o, (x + k) % 4, dz)
        for g in range(2) for o, dz in enumerate(GROUPS[g]) for k in range(4) if dz or k
    ]

    barrier = pltpu.get_barrier_semaphore()
    everyone = [at(y=v) for v in y_ids] + [at(c=1 - c)] + [at(x=v, z=(z + dz) % 8) for _, _, v, dz in plane]
    for other in everyone:
        pl.semaphore_signal(barrier, inc=1, device_id=other, device_id_type=MESH)

    loads = [
        pltpu.make_async_copy(src, dst, in_sem.at[i])
        for i, (src, dst) in enumerate(
            [(router_hbm, router), (patches_hbm, patches), (cot_hbm, cot), (w_in_hbm, w_in), (w_out_hbm, w_out)]
        )
    ]
    for load in loads:
        load.start()

    def send(src, dst, ssem, rsem, other):
        pltpu.make_async_remote_copy(
            src_ref=src, dst_ref=dst, send_sem=ssem, recv_sem=rsem, device_id=other, device_id_type=MESH
        ).start()

    def wait(ref, sem):
        pltpu.make_async_copy(ref, ref, sem).wait()

    def rows(start, size):
        return pl.ds(pl.multiple_of(start, size), size)

    def cols(k):
        return slice(k * W, (k + 1) * W)

    perm[0] = one_hot(M, M, lambda i: ((i // 4) % 4) * 64 + (i // 16) * 4 + i % 4)
    perm[1] = one_hot(M, M, lambda i: (i % 16) * 16 + i // 16)
    perm[2] = one_hot(M, M, lambda i: ((i // 4) % 16) * 16 + (i // 64) * 4 + i % 4)
    perm[3] = one_hot(M, M, lambda i: (i % 16) * 16 + i // 16)

    loads[0].wait()
    router_t[...] = dot_t(one_hot(E, E, lambda i: i), router[...]).astype(BF16)
    loads[1].wait()
    logits = dot_t(router_t[...], patches[...])
    e_d = jnp.exp(logits - jnp.max(logits, axis=1, keepdims=True))
    p_d = e_d / jnp.sum(e_d, axis=1, keepdims=True)
    prob_d[...] = p_d
    disp_t[0] = p_d.astype(BF16)

    def f0(p):
        rhs = patches if p == 0 else cot
        for k in range(4):
            part = dot(disp_t[p], rhs[:, cols(k)]).astype(BF16)
            for h in range(2):
                sr[p, h, k * 64:(k + 1) * 64] = part[h * 64:(h + 1) * 64]
        for h in range(2):
            ms[p, h * 16:(h + 1) * 16] = dot(perm[0], sr[p, h]).astype(BF16).reshape(16, 16, W)

    def f1(p):
        for g, o, v, dz in plane:
            to = (z + 8 - dz) % 8
            send(ms.at[p, to * 4 + v], xr.at[p, g, o * 4 + x], fs_sem.at[p, g, 0], fr_sem.at[p, g, 0], at(x=v, z=to))
        xr[p, 0, x] = ms[p, z * 4 + x]

    def f3(p, g):
        wait(xr.at[p, g, pl.ds(0, 15 + g)], fr_sem.at[p, g, 0])
        moved = dot(perm[1], xr[p, g].reshape(M, W)).astype(BF16)
        for k in range(4):
            for q in range(4):
                x4[p, g, q, :, cols(k)] = moved[(k * 4 + q) * 16:(k * 4 + q + 1) * 16]
        mine = rows(g * 128 + c * 64 + y * 16, 16)
        for v in y_ids:
            send(x4.at[p, g, pl.ds((v % 2) * 2, 2)], xf.at[p, :, mine], fs_sem.at[p, g, 1], fr_sem.at[p, g, 1], at(y=v))
        for s in range(2):
            xf[p, s, mine, :] = x4[p, g, yl * 2 + s]

    def f4(p, g):
        wait(xf.at[p, :, pl.ds(0, 48)], fr_sem.at[p, g, 1])
        half = xf.at[p, :, rows(g * 128 + c * 64, 64)]
        send(half, half, fs_sem.at[p, g, 2], fr_sem.at[p, g, 2], at(c=1 - c))

    def f5(p, g):
        wait(xf.at[p, :, pl.ds(0, 64)], fr_sem.at[p, g, 2])
        r = slice(g * 128, (g + 1) * 128)
        for s in range(2):
            if p == 0:
                pre[0, s, r] = dot(xf[0, s, r], w_in[s])
            else:
                pre[1, s, r] = dot_t(xf[1, s, r], w_out[s])

    def gelu(g):
        for s in range(2):
            def block(i, carry):
                r = rows(g * 128 + i * 32, 32)
                v = pre[0, s, r, :]
                t = jnp.tanh(GELU_COEF * (v + 0.044715 * v * v * v))
                hid[s, r, :] = (0.5 * v * (1.0 + t)).astype(BF16)
                slope[s, r, :] = 0.5 * (1.0 + t) + 0.5 * v * (1.0 - t * t) * GELU_COEF * (1.0 + 3.0 * 0.044715 * v * v)
                return carry
            lax.fori_loop(0, 4, block, 0)

    def grad_pre(g):
        for s in range(2):
            def block(i, carry):
                r = rows(g * 128 + i * 32, 32)
                gpre[s, r, :] = (pre[1, s, r, :] * slope[s, r, :]).astype(BF16)
                return carry
            lax.fori_loop(0, 4, block, 0)

    def g1(p, g):
        r = slice(g * 128, (g + 1) * 128)
        for s in range(2):
            if p == 0:
                po[p, g, s] = dot(hid[s, r], w_out[s])
            else:
                po[p, g, s] = dot_t(gpre[s, r], w_in[s])
            cs[p, g, s] = po[p, g, s, rows((1 - c) * 64, 64), :].astype(BF16)
        send(cs.at[p, g], cr.at[p, g], bs_sem.at[p, g, 0], br_sem.at[p, g, 0], at(c=1 - c))

    def g2(p, g):
        wait(cr.at[p, g], br_sem.at[p, g, 0])
        for s in range(2):
            total = (po[p, g, s, rows(c * 64, 64), :] + cr[p, g, s].astype(F32)).astype(BF16)
            for v in range(4):
                ys[p, g, v, s] = total[v * 16:(v + 1) * 16]
        for v in y_ids:
            send(ys.at[p, g, v], yr.at[p, g, y], bs_sem.at[p, g, 1], br_sem.at[p, g, 1], at(y=v))
        yr[p, g, y] = ys[p, g, y]

    def g3(p, g):
        wait(yr.at[p, g, pl.ds(0, 3)], br_sem.at[p, g, 1])
        total = (yr[p, g, 0:2].astype(F32) + yr[p, g, 2:4].astype(F32)).astype(BF16).reshape(64, D)
        stacked = jnp.concatenate([total[:, cols(k)] for k in range(4)], axis=0)
        zs[p, g] = dot(perm[3], stacked).astype(BF16).reshape(16, 16, W)
        for h, o, v, dz in plane:
            if h == g:
                to = (z + dz) % 8
                send(zs.at[p, g, o * 4 + v], zr.at[p, z * 4 + x], bs_sem.at[p, g, 2], br_sem.at[p, 0, 2], at(x=v, z=to))
        if g == 0:
            zr[p, z * 4 + x] = zs[p, 0, x]

    def g4(p):
        wait(zr.at[p, pl.ds(0, 31)], br_sem.at[p, 0, 2])
        for h in range(2):
            moved = dot(perm[2], zr[p, h * 16:(h + 1) * 16].reshape(M, W)).astype(BF16)
            for k in range(4):
                so[p, h * 64:(h + 1) * 64, cols(k)] = moved[k * 64:(k + 1) * 64]

    def w_out_grad(k):
        for s in range(2):
            gwo[s, :, cols(k)] = dot_tl(hid[s], xf[1, s, :, cols(k)]).astype(BF16)

    def w_in_grad(k):
        for s in range(2):
            gwi[s, cols(k), :] = dot_tl(xf[0, s, :, cols(k)], gpre[s]).astype(BF16)

    def combine_probs():
        e_c = jnp.exp(logits - jnp.max(logits, axis=0, keepdims=True))
        p_c = e_c / jnp.sum(e_c, axis=0, keepdims=True)
        prob_c[...] = p_c
        disp_t[1] = p_c.astype(BF16)

    def images_side():
        disp[...] = disp_t[0].T
        comb[...] = disp_t[1].T
        pick = one_hot(M, M, lambda i: ((i // 16) % 8) * 32 + ((i // 4) % 4) * 8 + (i // 128) * 4 + i % 4)
        for cc in range(2):
            for hh in range(2):
                pt[cc * 512 + hh * 256:cc * 512 + (hh + 1) * 256] = dot_t(
                    pick, patches[:, hh * 512 + cc * 256:hh * 512 + (cc + 1) * 256]
                ).astype(BF16)

    f0(0)
    pl.semaphore_wait(barrier, len(everyone))
    f1(0)
    combine_probs()
    loads[2].wait()
    f0(1)
    f1(1)
    images_side()
    f3(0, 0)
    f3(0, 1)
    f4(0, 0)
    loads[3].wait()
    f5(0, 0)
    gelu(0)
    f3(1, 0)
    f4(0, 1)
    loads[4].wait()
    g1(0, 0)
    f5(0, 1)
    gelu(1)
    g1(0, 1)
    f3(1, 1)
    g2(0, 0)
    f4(1, 0)
    g2(0, 1)
    f5(1, 0)
    grad_pre(0)
    g1(1, 0)
    f4(1, 1)
    g3(0, 0)
    g2(1, 0)
    f5(1, 1)
    grad_pre(1)
    g1(1, 1)
    g3(0, 1)
    g2(1, 1)
    w_out_grad(0)
    w_out_grad(1)
    g3(1, 0)
    w_out_grad(2)
    w_out_grad(3)
    g3(1, 1)
    w_in_grad(0)
    w_in_grad(1)
    g4(0)
    mixed[...] = dot(comb[...], so[0]).astype(BF16)
    p_c = prob_c[...]
    g_c = dot_t(so[0], cot[...])
    grad_c[...] = p_c * (g_c - jnp.sum(p_c * g_c, axis=0, keepdims=True))
    w_in_grad(2)
    w_in_grad(3)
    g4(1)
    p_d = prob_d[...]
    g_d = dot_t(so[1], patches[...])
    g_t = (grad_c[...] + p_d * (g_d - jnp.sum(p_d * g_d, axis=1, keepdims=True))).astype(BF16)

    rt[...] = dot_t(pt[...], g_t)
    rcs[...] = rt[rows((1 - c) * 512, 512), :].astype(BF16)
    send(rcs, rcr, rs_sem.at[0], rr_sem.at[0], at(c=1 - c))
    g_m = g_t.T
    for k in range(2):
        gp[:, cols(k)] = (dot(disp[...], so[1, :, cols(k)]) + dot(g_m, router_t[:, cols(k)])).astype(BF16)
    wait(rcr, rr_sem.at[0])
    rys[...] = (rt[rows(c * 512, 512), :] + rcr[...].astype(F32)).astype(BF16).reshape(4, 128, 128)
    for v in y_ids:
        send(rys.at[v], ryr.at[y], rs_sem.at[1], rr_sem.at[1], at(y=v))
    ryr[y] = rys[y]
    for k in range(2, 4):
        gp[:, cols(k)] = (dot(disp[...], so[1, :, cols(k)]) + dot(g_m, router_t[:, cols(k)])).astype(BF16)
    wait(ryr.at[pl.ds(0, 3)], rr_sem.at[1])
    total = jnp.sum(ryr[...].astype(F32), axis=0)
    for b in range(32):
        rzs[b] = total[b * 4:(b + 1) * 4]
    for g, o, v, dz in plane:
        to = (z + dz) % 8
        send(rzs.at[to * 4 + v], rzr.at[z * 4 + x], rs_sem.at[2], rr_sem.at[2], at(x=v, z=to))
    rzr[z * 4 + x] = rzs[z * 4 + x]
    wait(rzr.at[pl.ds(0, 31)], rr_sem.at[2])
    gr_ref[...] = jnp.sum(rzr[...], axis=0).astype(BF16)

    for p in range(2):
        for g in range(2):
            wait(xr.at[p, g, pl.ds(0, 15 + g)], fs_sem.at[p, g, 0])
            wait(xf.at[p, :, pl.ds(0, 48)], fs_sem.at[p, g, 1])
            wait(xf.at[p, :, pl.ds(0, 64)], fs_sem.at[p, g, 2])
            wait(cr.at[p, g], bs_sem.at[p, g, 0])
            wait(yr.at[p, g, pl.ds(0, 3)], bs_sem.at[p, g, 1])
            wait(zs.at[p, g, pl.ds(0, 15 + g)], bs_sem.at[p, g, 2])
    wait(rcr, rs_sem.at[0])
    wait(ryr.at[pl.ds(0, 3)], rs_sem.at[1])
    wait(rzr.at[pl.ds(0, 31)], rs_sem.at[2])


def store(*refs):
    sem = refs[-1]
    copies = [pltpu.make_async_copy(refs[i], refs[5 + i], sem.at[i]) for i in range(5)]
    for copy in copies:
        copy.start()
    for copy in copies:
        copy.wait()


def on_device(patches, router, w_in, w_out, cotangent):
    v = pltpu.VMEM
    any_spec = pl.BlockSpec(memory_space=pl.ANY)
    shapes = ((M, D), (M, D), (4, E), (2, D, FF), (2, FF, D))
    args = [
        pltpu.with_memory_space_constraint(a, pltpu.HBM)
        for a in (patches[0], router, w_in, w_out, cotangent[0])
    ]
    results = pl.pallas_call(
        kernel,
        name="soft_moe",
        out_shape=tuple(v(s, BF16) for s in shapes),
        in_specs=[any_spec] * 5,
        out_specs=[pl.BlockSpec(memory_space=pltpu.VMEM)] * 5,
        scratch_shapes=[
            v((M, D), BF16), v((D, E), BF16), v((2, D, FF), BF16), v((2, FF, D), BF16), v((M, D), BF16),
            v((4, M, M), BF16), v((D, M), BF16), v((E, D), BF16), v((E, M), F32), v((E, M), F32),
            v((2, E, M), BF16), v((M, E), BF16), v((M, E), BF16),
            v((2, 2, M, W), BF16), v((2, 32, 16, W), BF16), v((2, 2, 16, 16, W), BF16), v((2, 2, 4, 16, D), BF16),
            v((2, 2, 256, D), BF16),
            v((2, 2, 256, FF), F32), v((2, 256, FF), F32), v((2, 256, FF), BF16), v((2, 256, FF), BF16),
            v((2, 2, 2, 128, D), F32), v((2, 2, 2, 64, D), BF16), v((2, 2, 2, 64, D), BF16),
            v((2, 2, 4, 2, 16, D), BF16), v((2, 2, 4, 2, 16, D), BF16),
            v((2, 2, 16, 16, W), BF16), v((2, 32, 16, W), BF16), v((2, E, D), BF16),
            v((E, M), F32), v((E, M), F32),
            v((D, E), F32), v((512, E), BF16), v((512, E), BF16), v((4, 128, E), BF16), v((4, 128, E), BF16),
            v((32, 4, E), F32), v((32, 4, E), F32),
            pltpu.SemaphoreType.DMA((5,)),
            pltpu.SemaphoreType.DMA((2, 2, 3)), pltpu.SemaphoreType.DMA((2, 2, 3)),
            pltpu.SemaphoreType.DMA((2, 2, 3)), pltpu.SemaphoreType.DMA((2, 2, 3)),
            pltpu.SemaphoreType.DMA((3,)), pltpu.SemaphoreType.DMA((3,)),
        ],
        compiler_params=pltpu.CompilerParams(
            collective_id=0, has_side_effects=True, vmem_limit_bytes=44 * 2**20
        ),
        cost_estimate=pl.CostEstimate(flops=4_700_000_000, bytes_accessed=13_000_000, transcendentals=500_000),
    )(*args)
    mixed, gp, gr, gwi, gwo = pl.pallas_call(
        store,
        name="store",
        out_shape=tuple(jax.ShapeDtypeStruct(s, BF16) for s in shapes),
        in_specs=[pl.BlockSpec(memory_space=pltpu.VMEM)] * 5,
        out_specs=[any_spec] * 5,
        scratch_shapes=[pltpu.SemaphoreType.DMA((5,))],
        compiler_params=pltpu.CompilerParams(vmem_limit_bytes=4 * 2**20),
    )(*[pltpu.with_memory_space_constraint(a, pltpu.VMEM) for a in results])
    return mixed[None], gp[None], gr, gwi, gwo


def solution(mesh):
    placed = (
        P(("dp", "expert"), None, None),
        P(),
        P("expert", None, "dp"),
        P("expert", "dp", None),
        P(("dp", "expert"), None, None),
    )
    return jax.shard_map(
        on_device,
        mesh=mesh,
        in_specs=placed,
        out_specs=(
            P(("dp", "expert"), None, None),
            P(("dp", "expert"), None, None),
            P(("dp", "expert"), None),
            P("expert", None, "dp"),
            P("expert", "dp", None),
        ),
        check_vma=False,
    )
```

time: 352 us -> 73.6 us (0.21)
  blocking collectives: 233 us -> 0 us
  Pallas kernels: 0 us -> 72.9 us
  waiting for transfers between devices: 61.5 us -> 0 us
  matrix products: 29.9 us -> 0 us
  between operations: 13.9 us -> 0.64 us
  local copies, waits for them, and re-layouts: 12.2 us -> 0 us
    all_to_all x4 -> x0, blocking collectives: 154 us -> none  [the longest x2 113 us: to_images(): lax.all_to_all(partial_value, 'expert', split_axis=2, concat_axis=3, tile...]
    unnamed x1 -> x0, blocking collectives: 78.7 us -> none
    pallas_call x0 -> x2, Pallas kernels: none -> 72.9 us  [the longest x1 70.2 us: on_device(): pl.pallas_call(kernel, name='soft_moe', out_shape=tuple((v(s, BF16) for s...]
    reduce_scatter x2 -> x0, waiting for transfers between devices: 35.8 us -> none  [to_images(): summed = lax.psum_scatter(arrived, 'dp', scatter_dimension=0, tiled=True)]
    dot_general x15 -> x0, matrix products: 29.9 us -> none  [the longest x2 4.19 us: to_images(): jnp.einsum(pattern, operand, weight, preferred_element_type=jnp.float32)]
    all_gather x2 -> x0, waiting for transfers between devices: 25.6 us -> none  [to_experts(): gathered = lax.all_gather(arrived, 'dp', axis=0, tiled=True)]
    all_to_all x4 -> x0, local copies, waits for them, and re-layouts: 6.59 us -> none  [the longest x2 5.08 us: to_images(): lax.all_to_all(partial_value, 'expert', split_axis=2, concat_axis=3, tile...]
  transfers between devices with their start and end apart: 4 -> 0, of which waited for: 3 -> 0; matrix products, arithmetic and copies ran while one was open for 6% -> 0% of each run, Pallas kernels for 0% -> 0%
where the time goes in v2:
time: 73.6 us
  Pallas kernels  72.9 us (99%)
    pallas_call x1, Pallas kernels, on_device(): pl.pallas_call(kernel, name='soft_moe', out_shape=tuple((v(s, BF16) for s...  70.2 us
    pallas_call x1, Pallas kernels, on_device(): pl.pallas_call(store, name='store', out_shape=tuple((jax.ShapeDtypeStruct...  2.75 us

profile of v2, /device:TPU:1, one launch (start us, length us, event | category | flops | bytes accessed | tf_op | source)
XLA Modules:
  0.0 73.6 jit_solution(17601689419897145587)
XLA Ops:
  0.6 70.2 %soft_moe.1 = (bf16[256,1024]{1,0:T(8,128)(2,1)S(1)}, bf16[256,1024]{1,0:T(8,128)(2,1)S(1)}, bf16[4,128]{1,0:T(4,128)(2,1)S(1)}, bf16[2,1024,640]{2,1,0:T(8,128)(2,1)S(1)}, bf16[2,640,1024]{2,1,0:T(8,128)(2,1)S(1)}) custom-call(bf16[256,1024]{1,0:T(8,128)(2,1)} %bitcast.4, bf16[1024,128]{1,0:T(8,128)(2,1)} %router_hbm.1, bf16[2,1024,640]{2,1,0:T(8,128)(2,1)} %w_in_hbm.1, ...), custom_call_target="tpu_custom_call" | custom-call | flops 4700000256 | bytes 13000000 | tf_op jit(solution)/shard_map/soft_moe/pallas_call | solution.py:339
  70.8 2.8 %store.1 = (bf16[256,1024]{1,0:T(8,128)(2,1)}, bf16[256,1024]{1,0:T(8,128)(2,1)}, bf16[4,128]{1,0:T(4,128)(2,1)}, bf16[2,1024,640]{2,1,0:T(8,128)(2,1)}, bf16[2,640,1024]{2,1,0:T(8,128)(2,1)}) custom-call(bf16[256,1024]{1,0:T(8,128)(2,1)S(1)} %get-tuple-element.15.refs_0_, bf16[256,1024]{1,0:T(8,128)(2,1)S(1)} %get-tuple-element.16.refs_1_, ...), custom_call_target="tpu_custom_call" | custom-call | tf_op jit(solution)/shard_map/store/pallas_call | solution.py:368

commit v3 on v2

--- a/solution.py
+++ b/solution.py
@@ -40,9 +40,9 @@
     patches_hbm, router_hbm, w_in_hbm, w_out_hbm, cot_hbm,
     mixed, gp, gr_ref, gwi, gwo,
     patches, router, w_in, w_out, cot,
-    perm, pt, router_t, prob_d, prob_c, disp_t, disp, comb,
+    perm, pt, prob_d, prob_c, disp_t, disp, comb,
     sr, ms, xr, x4, xf, pre, slope, hid, gpre,
-    po, cs, cr, ys, yr, zs, zr, so, grad_c, grad_d,
+    po, cs, cr, ys, yr, zs, zr, so, grad_c,
     rt, rcs, rcr, rys, ryr, rzs, rzr,
     in_sem, fs_sem, fr_sem, bs_sem, br_sem, rs_sem, rr_sem,
 ):
@@ -72,7 +72,7 @@
             [(router_hbm, router), (patches_hbm, patches), (cot_hbm, cot), (w_in_hbm, w_in), (w_out_hbm, w_out)]
         )
     ]
-    for load in loads:
+    for load in loads[:3]:
         load.start()
 
     def send(src, dst, ssem, rsem, other):
@@ -95,13 +95,13 @@
     perm[3] = one_hot(M, M, lambda i: (i % 16) * 16 + i // 16)
 
     loads[0].wait()
-    router_t[...] = dot_t(one_hot(E, E, lambda i: i), router[...]).astype(BF16)
     loads[1].wait()
-    logits = dot_t(router_t[...], patches[...])
-    e_d = jnp.exp(logits - jnp.max(logits, axis=1, keepdims=True))
-    p_d = e_d / jnp.sum(e_d, axis=1, keepdims=True)
+    logits = dot(patches[...], router[...])
+    e_d = jnp.exp(logits - jnp.max(logits, axis=0, keepdims=True))
+    p_d = e_d / jnp.sum(e_d, axis=0, keepdims=True)
     prob_d[...] = p_d
-    disp_t[0] = p_d.astype(BF16)
+    disp[...] = p_d.astype(BF16)
+    disp_t[0] = disp[...].T
 
     def f0(p):
         rhs = patches if p == 0 else cot
@@ -211,14 +211,13 @@
             gwi[s, cols(k), :] = dot_tl(xf[0, s, :, cols(k)], gpre[s]).astype(BF16)
 
     def combine_probs():
-        e_c = jnp.exp(logits - jnp.max(logits, axis=0, keepdims=True))
-        p_c = e_c / jnp.sum(e_c, axis=0, keepdims=True)
+        e_c = jnp.exp(logits - jnp.max(logits, axis=1, keepdims=True))
+        p_c = e_c / jnp.sum(e_c, axis=1, keepdims=True)
         prob_c[...] = p_c
-        disp_t[1] = p_c.astype(BF16)
+        comb[...] = p_c.astype(BF16)
+        disp_t[1] = comb[...].T
 
     def images_side():
-        disp[...] = disp_t[0].T
-        comb[...] = disp_t[1].T
         pick = one_hot(M, M, lambda i: ((i // 16) % 8) * 32 + ((i // 4) % 4) * 8 + (i // 128) * 4 + i % 4)
         for cc in range(2):
             for hh in range(2):
@@ -229,72 +228,73 @@
     f0(0)
     pl.semaphore_wait(barrier, len(everyone))
     f1(0)
+    for load in loads[3:]:
+        load.start()
     combine_probs()
     loads[2].wait()
     f0(1)
-    f1(1)
     images_side()
     f3(0, 0)
+    f1(1)
     f3(0, 1)
     f4(0, 0)
+    f3(1, 0)
     loads[3].wait()
     f5(0, 0)
     gelu(0)
-    f3(1, 0)
-    f4(0, 1)
     loads[4].wait()
     g1(0, 0)
+    f4(0, 1)
+    f3(1, 1)
+    g2(0, 0)
     f5(0, 1)
     gelu(1)
     g1(0, 1)
-    f3(1, 1)
-    g2(0, 0)
     f4(1, 0)
     g2(0, 1)
     f5(1, 0)
     grad_pre(0)
+    f4(1, 1)
     g1(1, 0)
-    f4(1, 1)
-    g3(0, 0)
-    g2(1, 0)
     f5(1, 1)
     grad_pre(1)
+    g2(1, 0)
     g1(1, 1)
+    g3(0, 0)
+    g2(1, 1)
     g3(0, 1)
-    g2(1, 1)
     w_out_grad(0)
     w_out_grad(1)
-    g3(1, 0)
     w_out_grad(2)
     w_out_grad(3)
-    g3(1, 1)
+    g3(1, 0)
     w_in_grad(0)
     w_in_grad(1)
+    g3(1, 1)
+    w_in_grad(2)
+    w_in_grad(3)
     g4(0)
     mixed[...] = dot(comb[...], so[0]).astype(BF16)
     p_c = prob_c[...]
-    g_c = dot_t(so[0], cot[...])
-    grad_c[...] = p_c * (g_c - jnp.sum(p_c * g_c, axis=0, keepdims=True))
-    w_in_grad(2)
-    w_in_grad(3)
+    g_c = dot_t(cot[...], so[0])
+    grad_c[...] = p_c * (g_c - jnp.sum(p_c * g_c, axis=1, keepdims=True))
     g4(1)
     p_d = prob_d[...]
-    g_d = dot_t(so[1], patches[...])
-    g_t = (grad_c[...] + p_d * (g_d - jnp.sum(p_d * g_d, axis=1, keepdims=True))).astype(BF16)
-
-    rt[...] = dot_t(pt[...], g_t)
-    rcs[...] = rt[rows((1 - c) * 512, 512), :].astype(BF16)
+    g_d = dot_t(patches[...], so[1])
+    g_m = (grad_c[...] + p_d * (g_d - jnp.sum(p_d * g_d, axis=0, keepdims=True))).astype(BF16)
+
+    rcs[...] = dot(pt[rows((1 - c) * 512, 512), :], g_m).astype(BF16)
     send(rcs, rcr, rs_sem.at[0], rr_sem.at[0], at(c=1 - c))
-    g_m = g_t.T
+    rt[...] = dot(pt[rows(c * 512, 512), :], g_m)
     for k in range(2):
-        gp[:, cols(k)] = (dot(disp[...], so[1, :, cols(k)]) + dot(g_m, router_t[:, cols(k)])).astype(BF16)
+        gp[:, cols(k)] = (dot(disp[...], so[1, :, cols(k)]) + dot_t(g_m, router[cols(k), :])).astype(BF16)
     wait(rcr, rr_sem.at[0])
-    rys[...] = (rt[rows(c * 512, 512), :] + rcr[...].astype(F32)).astype(BF16).reshape(4, 128, 128)
+    rys[...] = (rt[...] + rcr[...].astype(F32)).astype(BF16).reshape(4, 128, 128)
     for v in y_ids:
         send(rys.at[v], ryr.at[y], rs_sem.at[1], rr_sem.at[1], at(y=v))
     ryr[y] = rys[y]
     for k in range(2, 4):
-        gp[:, cols(k)] = (dot(disp[...], so[1, :, cols(k)]) + dot(g_m, router_t[:, cols(k)])).astype(BF16)
+        gp[:, cols(k)] = (dot(disp[...], so[1, :, cols(k)]) + dot_t(g_m, router[cols(k), :])).astype(BF16)
     wait(ryr.at[pl.ds(0, 3)], rr_sem.at[1])
     total = jnp.sum(ryr[...].astype(F32), axis=0)
     for b in range(32):
@@ -321,9 +321,16 @@
 
 def store(*refs):
     sem = refs[-1]
-    copies = [pltpu.make_async_copy(refs[i], refs[5 + i], sem.at[i]) for i in range(5)]
-    for copy in copies:
-        copy.start()
+    copies = []
+    for src, dst in zip(refs[:5], refs[5:10]):
+        if src.shape[0] == 2:
+            parts = [(src.at[s, pl.ds(h, src.shape[1] // 2)], dst.at[s, pl.ds(h, src.shape[1] // 2)])
+                     for s in range(2) for h in (0, src.shape[1] // 2)]
+        else:
+            parts = [(src, dst)]
+        for a, b in parts:
+            copies.append(pltpu.make_async_copy(a, b, sem.at[len(copies)]))
+            copies[-1].start()
     for copy in copies:
         copy.wait()
 
@@ -344,7 +351,7 @@
         out_specs=[pl.BlockSpec(memory_space=pltpu.VMEM)] * 5,
         scratch_shapes=[
             v((M, D), BF16), v((D, E), BF16), v((2, D, FF), BF16), v((2, FF, D), BF16), v((M, D), BF16),
-            v((4, M, M), BF16), v((D, M), BF16), v((E, D), BF16), v((E, M), F32), v((E, M), F32),
+            v((4, M, M), BF16), v((D, M), BF16), v((M, E), F32), v((M, E), F32),
             v((2, E, M), BF16), v((M, E), BF16), v((M, E), BF16),
             v((2, 2, M, W), BF16), v((2, 32, 16, W), BF16), v((2, 2, 16, 16, W), BF16), v((2, 2, 4, 16, D), BF16),
             v((2, 2, 256, D), BF16),
@@ -352,8 +359,8 @@
             v((2, 2, 2, 128, D), F32), v((2, 2, 2, 64, D), BF16), v((2, 2, 2, 64, D), BF16),
             v((2, 2, 4, 2, 16, D), BF16), v((2, 2, 4, 2, 16, D), BF16),
             v((2, 2, 16, 16, W), BF16), v((2, 32, 16, W), BF16), v((2, E, D), BF16),
-            v((E, M), F32), v((E, M), F32),
-            v((D, E), F32), v((512, E), BF16), v((512, E), BF16), v((4, 128, E), BF16), v((4, 128, E), BF16),
+            v((M, E), F32),
+            v((512, E), F32), v((512, E), BF16), v((512, E), BF16), v((4, 128, E), BF16), v((4, 128, E), BF16),
             v((32, 4, E), F32), v((32, 4, E), F32),
             pltpu.SemaphoreType.DMA((5,)),
             pltpu.SemaphoreType.DMA((2, 2, 3)), pltpu.SemaphoreType.DMA((2, 2, 3)),
@@ -371,7 +378,7 @@
         out_shape=tuple(jax.ShapeDtypeStruct(s, BF16) for s in shapes),
         in_specs=[pl.BlockSpec(memory_space=pltpu.VMEM)] * 5,
         out_specs=[any_spec] * 5,
-        scratch_shapes=[pltpu.SemaphoreType.DMA((5,))],
+        scratch_shapes=[pltpu.SemaphoreType.DMA((11,))],
         compiler_params=pltpu.CompilerParams(vmem_limit_bytes=4 * 2**20),
     )(*[pltpu.with_memory_space_constraint(a, pltpu.VMEM) for a in results])
     return mixed[None], gp[None], gr, gwi, gwo

time: 73.6 us -> 70.5 us (0.958)
  Pallas kernels: 72.9 us -> 69.8 us
    pallas_call x1, Pallas kernels: 70.2 us -> 67 us  [on_device(): pl.pallas_call(kernel, name='soft_moe', out_shape=tuple((v(s, BF16) for s...]
where the time goes in v3:
time: 70.5 us; the launch traced here: 70.4 us
  Pallas kernels  69.8 us (99%)
    pallas_call x1, Pallas kernels, on_device(): pl.pallas_call(kernel, name='soft_moe', out_shape=tuple((v(s, BF16) for s...  67 us
    pallas_call x1, Pallas kernels, on_device(): pl.pallas_call(store, name='store', out_shape=tuple((jax.ShapeDtypeStruct...  2.76 us

profile of v3, /device:TPU:1, one launch (start us, length us, event | category | flops | bytes accessed | tf_op | source)
XLA Modules:
  0.0 70.4 jit_solution(10052416979270497814)
XLA Ops:
  0.6 67.0 %soft_moe.1 = (bf16[256,1024]{1,0:T(8,128)(2,1)S(1)}, bf16[256,1024]{1,0:T(8,128)(2,1)S(1)}, bf16[4,128]{1,0:T(4,128)(2,1)S(1)}, bf16[2,1024,640]{2,1,0:T(8,128)(2,1)S(1)}, bf16[2,640,1024]{2,1,0:T(8,128)(2,1)S(1)}) custom-call(bf16[256,1024]{1,0:T(8,128)(2,1)} %bitcast.4, bf16[1024,128]{1,0:T(8,128)(2,1)} %router_hbm.1, bf16[2,1024,640]{2,1,0:T(8,128)(2,1)} %w_in_hbm.1, ...), custom_call_target="tpu_custom_call" | custom-call | flops 4700000256 | bytes 13000000 | tf_op jit(solution)/shard_map/soft_moe/pallas_call | solution.py:346
  67.7 2.8 %store.1 = (bf16[256,1024]{1,0:T(8,128)(2,1)}, bf16[256,1024]{1,0:T(8,128)(2,1)}, bf16[4,128]{1,0:T(4,128)(2,1)}, bf16[2,1024,640]{2,1,0:T(8,128)(2,1)}, bf16[2,640,1024]{2,1,0:T(8,128)(2,1)}) custom-call(bf16[256,1024]{1,0:T(8,128)(2,1)S(1)} %get-tuple-element.15.refs_0_, bf16[256,1024]{1,0:T(8,128)(2,1)S(1)} %get-tuple-element.16.refs_1_, ...), custom_call_target="tpu_custom_call" | custom-call | tf_op jit(solution)/shard_map/store/pallas_call | solution.py:375

commit v4 on v3

--- a/solution.py
+++ b/solution.py
@@ -33,7 +33,8 @@
     return jnp.where(old_of_new(new) == old, 1.0, 0.0).astype(BF16)
 
 
-GROUPS = ((0, 1, 7, 2), (6, 3, 5, 4))
+GROUPS = ((2, 7, 1, 0), (4, 3, 5, 6))
+HOME = [(g, o) for g in range(2) for o in range(4) if GROUPS[g][o] == 0][0]
 
 
 def kernel(
@@ -55,10 +56,10 @@
     def at(x=x, y=y, z=z, c=c):
         return {"dp": (y // 2) * 2 + c, "expert": (z * 4 + x) * 2 + y % 2}
 
-    y_ids = [(y + k) % 4 for k in range(1, 4)]
+    y_ids = [(y + k) % 4 for k in (1, 3, 2)]
     plane = [
         (g, o, (x + k) % 4, dz)
-        for g in range(2) for o, dz in enumerate(GROUPS[g]) for k in range(4) if dz or k
+        for g in range(2) for o, dz in enumerate(GROUPS[g]) for k in (2, 1, 3, 0) if dz or k
     ]
 
     barrier = pltpu.get_barrier_semaphore()
@@ -116,24 +117,26 @@
         for g, o, v, dz in plane:
             to = (z + 8 - dz) % 8
             send(ms.at[p, to * 4 + v], xr.at[p, g, o * 4 + x], fs_sem.at[p, g, 0], fr_sem.at[p, g, 0], at(x=v, z=to))
-        xr[p, 0, x] = ms[p, z * 4 + x]
+        xr[p, HOME[0], HOME[1] * 4 + x] = ms[p, z * 4 + x]
 
     def f3(p, g):
-        wait(xr.at[p, g, pl.ds(0, 15 + g)], fr_sem.at[p, g, 0])
+        wait(xr.at[p, g, pl.ds(0, 16 - (g == HOME[0]))], fr_sem.at[p, g, 0])
         moved = dot(perm[1], xr[p, g].reshape(M, W)).astype(BF16)
         for k in range(4):
             for q in range(4):
                 x4[p, g, q, :, cols(k)] = moved[(k * 4 + q) * 16:(k * 4 + q + 1) * 16]
         mine = rows(g * 128 + c * 64 + y * 16, 16)
-        for v in y_ids:
-            send(x4.at[p, g, pl.ds((v % 2) * 2, 2)], xf.at[p, :, mine], fs_sem.at[p, g, 1], fr_sem.at[p, g, 1], at(y=v))
-        for s in range(2):
+        for s in range(2):
+            for v in y_ids:
+                send(x4.at[p, g, (v % 2) * 2 + s], xf.at[p, s, mine], fs_sem.at[p, g, 1], fr_sem.at[p, g, 1], at(y=v))
             xf[p, s, mine, :] = x4[p, g, yl * 2 + s]
+        send(x4.at[p, g, pl.ds(yl * 2, 2)], xf.at[p, :, mine], fs_sem.at[p, g, 2], fr_sem.at[p, g, 2], at(c=1 - c))
 
     def f4(p, g):
         wait(xf.at[p, :, pl.ds(0, 48)], fr_sem.at[p, g, 1])
-        half = xf.at[p, :, rows(g * 128 + c * 64, 64)]
-        send(half, half, fs_sem.at[p, g, 2], fr_sem.at[p, g, 2], at(c=1 - c))
+        for v in y_ids:
+            part = xf.at[p, :, rows(g * 128 + c * 64 + v * 16, 16)]
+            send(part, part, fs_sem.at[p, g, 2], fr_sem.at[p, g, 2], at(c=1 - c))
 
     def f5(p, g):
         wait(xf.at[p, :, pl.ds(0, 64)], fr_sem.at[p, g, 2])
@@ -179,8 +182,9 @@
             total = (po[p, g, s, rows(c * 64, 64), :] + cr[p, g, s].astype(F32)).astype(BF16)
             for v in range(4):
                 ys[p, g, v, s] = total[v * 16:(v + 1) * 16]
-        for v in y_ids:
-            send(ys.at[p, g, v], yr.at[p, g, y], bs_sem.at[p, g, 1], br_sem.at[p, g, 1], at(y=v))
+        for s in range(2):
+            for v in y_ids:
+                send(ys.at[p, g, v, s], yr.at[p, g, y, s], bs_sem.at[p, g, 1], br_sem.at[p, g, 1], at(y=v))
         yr[p, g, y] = ys[p, g, y]
 
     def g3(p, g):
@@ -192,8 +196,8 @@
             if h == g:
                 to = (z + dz) % 8
                 send(zs.at[p, g, o * 4 + v], zr.at[p, z * 4 + x], bs_sem.at[p, g, 2], br_sem.at[p, 0, 2], at(x=v, z=to))
-        if g == 0:
-            zr[p, z * 4 + x] = zs[p, 0, x]
+        if g == HOME[0]:
+            zr[p, z * 4 + x] = zs[p, g, HOME[1] * 4 + x]
 
     def g4(p):
         wait(zr.at[p, pl.ds(0, 31)], br_sem.at[p, 0, 2])
@@ -286,15 +290,11 @@
     rcs[...] = dot(pt[rows((1 - c) * 512, 512), :], g_m).astype(BF16)
     send(rcs, rcr, rs_sem.at[0], rr_sem.at[0], at(c=1 - c))
     rt[...] = dot(pt[rows(c * 512, 512), :], g_m)
-    for k in range(2):
-        gp[:, cols(k)] = (dot(disp[...], so[1, :, cols(k)]) + dot_t(g_m, router[cols(k), :])).astype(BF16)
     wait(rcr, rr_sem.at[0])
     rys[...] = (rt[...] + rcr[...].astype(F32)).astype(BF16).reshape(4, 128, 128)
     for v in y_ids:
         send(rys.at[v], ryr.at[y], rs_sem.at[1], rr_sem.at[1], at(y=v))
     ryr[y] = rys[y]
-    for k in range(2, 4):
-        gp[:, cols(k)] = (dot(disp[...], so[1, :, cols(k)]) + dot_t(g_m, router[cols(k), :])).astype(BF16)
     wait(ryr.at[pl.ds(0, 3)], rr_sem.at[1])
     total = jnp.sum(ryr[...].astype(F32), axis=0)
     for b in range(32):
@@ -303,17 +303,19 @@
         to = (z + dz) % 8
         send(rzs.at[to * 4 + v], rzr.at[z * 4 + x], rs_sem.at[2], rr_sem.at[2], at(x=v, z=to))
     rzr[z * 4 + x] = rzs[z * 4 + x]
+    for k in range(4):
+        gp[:, cols(k)] = (dot(disp[...], so[1, :, cols(k)]) + dot_t(g_m, router[cols(k), :])).astype(BF16)
     wait(rzr.at[pl.ds(0, 31)], rr_sem.at[2])
     gr_ref[...] = jnp.sum(rzr[...], axis=0).astype(BF16)
 
     for p in range(2):
         for g in range(2):
-            wait(xr.at[p, g, pl.ds(0, 15 + g)], fs_sem.at[p, g, 0])
+            wait(xr.at[p, g, pl.ds(0, 16 - (g == HOME[0]))], fs_sem.at[p, g, 0])
             wait(xf.at[p, :, pl.ds(0, 48)], fs_sem.at[p, g, 1])
             wait(xf.at[p, :, pl.ds(0, 64)], fs_sem.at[p, g, 2])
             wait(cr.at[p, g], bs_sem.at[p, g, 0])
             wait(yr.at[p, g, pl.ds(0, 3)], bs_sem.at[p, g, 1])
-            wait(zs.at[p, g, pl.ds(0, 15 + g)], bs_sem.at[p, g, 2])
+            wait(zs.at[p, g, pl.ds(0, 16 - (g == HOME[0]))], bs_sem.at[p, g, 2])
     wait(rcr, rs_sem.at[0])
     wait(ryr.at[pl.ds(0, 3)], rs_sem.at[1])
     wait(rzr.at[pl.ds(0, 31)], rs_sem.at[2])

time: 70.5 us -> 67.8 us (0.962)
  Pallas kernels: 69.8 us -> 66.9 us
    pallas_call x1, Pallas kernels: 67 us -> 64.1 us  [on_device(): pl.pallas_call(kernel, name='soft_moe', out_shape=tuple((v(s, BF16) for s...]
where the time goes in v4:
time: 67.8 us; the launch traced here: 67.7 us
  Pallas kernels  66.9 us (99%)
  between operations  0.8 us (1%)
    pallas_call x1, Pallas kernels, on_device(): pl.pallas_call(kernel, name='soft_moe', out_shape=tuple((v(s, BF16) for s...  64.1 us
    pallas_call x1, Pallas kernels, on_device(): pl.pallas_call(store, name='store', out_shape=tuple((jax.ShapeDtypeStruct...  2.76 us

profile of v4, /device:TPU:1, one launch (start us, length us, event | category | flops | bytes accessed | tf_op | source)
XLA Modules:
  0.0 67.7 jit_solution(3129072036875664070)
XLA Ops:
  0.6 64.1 %soft_moe.1 = (bf16[256,1024]{1,0:T(8,128)(2,1)S(1)}, bf16[256,1024]{1,0:T(8,128)(2,1)S(1)}, bf16[4,128]{1,0:T(4,128)(2,1)S(1)}, bf16[2,1024,640]{2,1,0:T(8,128)(2,1)S(1)}, bf16[2,640,1024]{2,1,0:T(8,128)(2,1)S(1)}) custom-call(bf16[256,1024]{1,0:T(8,128)(2,1)} %bitcast.4, bf16[1024,128]{1,0:T(8,128)(2,1)} %router_hbm.1, bf16[2,1024,640]{2,1,0:T(8,128)(2,1)} %w_in_hbm.1, ...), custom_call_target="tpu_custom_call" | custom-call | flops 4700000256 | bytes 13000000 | tf_op jit(solution)/shard_map/soft_moe/pallas_call | solution.py:348
  64.8 2.8 %store.1 = (bf16[256,1024]{1,0:T(8,128)(2,1)}, bf16[256,1024]{1,0:T(8,128)(2,1)}, bf16[4,128]{1,0:T(4,128)(2,1)}, bf16[2,1024,640]{2,1,0:T(8,128)(2,1)}, bf16[2,640,1024]{2,1,0:T(8,128)(2,1)}) custom-call(bf16[256,1024]{1,0:T(8,128)(2,1)S(1)} %get-tuple-element.15.refs_0_, bf16[256,1024]{1,0:T(8,128)(2,1)S(1)} %get-tuple-element.16.refs_1_, ...), custom_call_target="tpu_custom_call" | custom-call | tf_op jit(solution)/shard_map/store/pallas_call | solution.py:377
